TPU v7x, 32 devices: a whole 2x2x4 slice. The times are simulated.
32 devices in a mesh: groups: 2 (over x), tensor: 8 (over z, y), store: 2 (over core).
Axes of the slice: x: 2, y: 2, z: 4, core: 2. Of those that a mesh axis runs over, the one named last changes fastest.
Arguments:
- activations: bfloat16 [8192, 28672], P(('groups', 'store'), 'tensor'), parts along dimension 0, may hold values from -6 to 6
- out_grads: bfloat16 [8192, 8192], P(('groups', 'store', 'tensor')), parts along dimension 0, may hold values from -6 to 6
- factor_in: bfloat16 [28672, 64], P('tensor'), may hold values from -0.03125 to 0.03125
- factor_out: bfloat16 [8192, 64], replicated, may hold values from -0.0625 to 0.0625
- store_rows: bfloat16 [49152, 4096], P(('groups', 'tensor', 'store')), parts along dimension 0, may hold values from -0.09375 to 0.09375
Outputs:
- scores: float32 [32, 24576], P('groups', ('tensor', 'store')), parts along dimension 0
There are 2 independent parts, one for each index of `groups`. A program takes and returns all parts, laid end to end along the dimension named above; an argument that names none is the same for every part. Nothing has to cross between parts.
All inputs are finite; a program needn't handle non-finite values.
Results may differ from a plain program's by a relative error of at most 0.0095.
Values may be sent and summed in bfloat16 or wider, within the bound.
A program may use at most 128 MiB of HBM per device.

v0:
```python
import jax
import jax.numpy as jnp
from jax import lax
from jax.sharding import PartitionSpec as P

RANK = 64
UTT_LEN = 256


def shards(activations, out_grads, factor_in, factor_out, store_rows):
    proj_in = jnp.dot(activations, factor_in, preferred_element_type=jnp.float32)
    proj_out = jnp.dot(out_grads, factor_out, preferred_element_type=jnp.float32)
    count = activations.shape[0] // UTT_LEN
    factor = 1.0 / jnp.sqrt(jnp.float32(UTT_LEN))
    summed = lax.psum(proj_in, "tensor")
    outer_all = lax.all_gather(proj_out, "tensor", axis=0, tiled=True)
    sketch = (
        jnp.einsum(
            "qta,qtb->qab",
            outer_all.reshape(count, UTT_LEN, RANK),
            summed.reshape(count, UTT_LEN, RANK),
        )
        * factor
    )
    sketch = sketch.reshape(count, RANK * RANK)
    every_sketch = lax.all_gather(sketch.astype(jnp.bfloat16), "store", axis=0, tiled=True)
    return lax.dot_general(
        every_sketch, store_rows, (((1,), (1,)), ((), ())), preferred_element_type=jnp.float32
    )


def solution(mesh):
    in_specs = (
        P(("groups", "store"), "tensor"),
        P(("groups", "store", "tensor"), None),
        P("tensor", None),
        P(),
        P(("groups", "tensor", "store"), None),
    )
    out_specs = P("groups", ("tensor", "store"))
    return jax.shard_map(shards, mesh=mesh, in_specs=in_specs, out_specs=out_specs, check_vma=False)
```

profile of v0, /device:TPU:0, one launch (start us, length us, event | category | flops | bytes accessed | tf_op | source)
XLA Modules:
  0.0 100.3 jit_solution(973321133490288768)
XLA Ops:
  0.0 0.0 copy-start
  0.0 9.8 %fusion.4 = f32[2048,64]{0,1:T(8,128)S(1)} fusion(bf16[2048,3584]{1,0:T(8,128)(2,1)} %param.5, bf16[3584,64]{0,1:T(8,128)(2,1)} %param.7), kind=kOutput, calls=%fused_computation.6 | convolution fusion | flops 939524096 | bytes 15663104 | tf_op jit(solution)/shard_map/dot_general | solution.py:11
  9.8 45.2 %all-reduce.1 = bf16[8,256,64]{1,2,0:T(8,128)(2,1)S(1)} all-reduce(f32[8,256,64]{1,2,0:T(8,128)S(1)} %bitcast.16), channel_id=1, replica_groups=mesh['groups'=2,'tensor'=8,'store'=2] {'tensor'}, use_global_device_ids=true, to_apply=%region_0.0 | all-reduce | flops 131072 | bytes 786432 | tf_op jit(solution)/shard_map/psum | solution.py:15
  55.1 0.0 copy-done
  55.1 3.6 %fusion.3 = bf16[256,64]{0,1:T(8,128)(2,1)S(1)} fusion(bf16[256,8192]{1,0:T(8,128)(2,1)} %param.6, bf16[8192,64]{0,1:T(8,128)(2,1)S(1)} %copy-done), kind=kOutput, calls=%fused_computation.5 | convolution fusion | flops 268435456 | bytes 5275648 | tf_op jit(solution)/shard_map/dot_general | solution.py:12
  58.7 30.7 %all_gather.6 = bf16[2048,64]{0,1:T(8,128)(2,1)S(1)} all-gather(bf16[256,64]{0,1:T(8,128)(2,1)S(1)} %fusion.3), channel_id=1, replica_groups=mesh['groups'=2,'tensor'=8,'store'=2] {'tensor'}, dimensions={0}, use_global_device_ids=true | all-gather | bytes 294912 | tf_op jit(solution)/shard_map/all_gather | solution.py:16
  89.4 0.2 fusion
  89.6 0.2 convert_element_type.7
  89.8 1.9 %all_gather.7 = bf16[16,4096]{1,0:T(8,128)(2,1)S(1)} all-gather(bf16[8,4096]{1,0:T(8,128)(2,1)S(1)} %convert_element_type.7), channel_id=1, replica_groups=mesh['groups'=2,'tensor'=8,'store'=2] {'store'}, dimensions={0}, use_global_device_ids=true | all-gather | bytes 196608 | tf_op jit(solution)/shard_map/all_gather | solution.py:26
  91.7 8.6 %fusion.5 = f32[16,1536]{1,0:T(8,128)} fusion(bf16[16,4096]{1,0:T(8,128)(2,1)S(1)} %all_gather.7, bf16[1536,4096]{1,0:T(8,128)(2,1)} %param.9), kind=kOutput, calls=%fused_computation.7 | convolution fusion | flops 201326592 | bytes 12812288 | tf_op jit(solution)/shard_map/dot_general | solution.py:27
  (1 shorter events, 0.0 us)
Async XLA Ops:
  0.0 55.1 %copy-start = (bf16[8192,64]{0,1:T(8,128)(2,1)S(1)}, bf16[8192,64]{0,1:T(8,128)(2,1)}, u32[]{:S(2)}) copy-start(bf16[8192,64]{0,1:T(8,128)(2,1)} %param.8) | copy-start | bytes 3145732
where the time goes:
time: 101 us; the launch traced here: 100 us
  blocking collectives  77.9 us (77%)
  matrix products  22.1 us (22%)
    psum x1, blocking collectives, shards(): summed = lax.psum(proj_in, 'tensor')  45.2 us
    all_gather x1, blocking collectives, shards(): outer_all = lax.all_gather(proj_out, 'tensor', axis=0, tiled=True)  30.7 us
    dot_general x1, matrix products, shards(): jnp.dot(activations, factor_in, preferred_element_type=jnp.float32)  9.77 us
    dot_general x1, matrix products, shards(): lax.dot_general(every_sketch, store_rows, (((1,), (1,)), ((), ())), prefe...  8.57 us
    dot_general x1, matrix products, shards(): jnp.dot(out_grads, factor_out, preferred_element_type=jnp.float32)  3.58 us

commit v1 on v0

v1 whole, which is shorter than its diff:
```python
import functools

import jax
import jax.numpy as jnp
from jax import lax
from jax.experimental import pallas as pl
from jax.experimental.pallas import tpu as pltpu
from jax.sharding import PartitionSpec as P

RANK = 64
UTT_LEN = 256
PACK = 128 // RANK
STORE_CHUNKS = 4
GRAD_CHUNKS = 2
FORWARD_AFTER = 4
MESH = pl.DeviceIdType.MESH
NT = (((1,), (1,)), ((), ()))


def dot_nt(a, b):
    return lax.dot_general(a, b, NT, preferred_element_type=jnp.float32)


def kernel(
    T, S,
    act, grads, fin, fout, rows, out,
    act_v, grads_v, fin_v, fout_v, rows_v, proj_v, outer_v, part_v, send_v, recv_v, every_v, wide_v, sk_v, tmp_v,
    act_sem, grads_sem, fin_sem, fout_sem, rows_sem,
    g_send, g_recv, r_send, r_recv, e_send, e_recv,
):
    t = lax.axis_index("tensor")
    s = lax.axis_index("store")
    tokens = act.shape[0]
    count = tokens // UTT_LEN
    block = grads.shape[0]
    own = count * RANK // T
    packed = own // PACK
    lo, hi = lax.rem(t, 2), t // 2

    width = grads.shape[1] // GRAD_CHUNKS
    loads_g = []
    for c in range(GRAD_CHUNKS):
        cols = pl.ds(c * width, width)
        loads_g.append((
            pltpu.make_async_copy(fout.at[:, cols], fout_v.at[:, cols], fout_sem.at[c]),
            pltpu.make_async_copy(grads.at[:, cols], grads_v.at[:, cols], grads_sem.at[c]),
        ))
    for a, b in loads_g:
        a.start()
        b.start()
    loads_f = [
        pltpu.make_async_copy(fin, fin_v.at[pl.ds(i * RANK, RANK), :], fin_sem.at[i]) for i in range(PACK)
    ]
    for c in loads_f:
        c.start()

    def act_copy(q):
        r = pl.ds(pl.multiple_of(q * UTT_LEN, UTT_LEN), UTT_LEN)
        return pltpu.make_async_copy(act.at[r, :], act_v.at[r, :], act_sem.at[q])

    for q in range(count):
        act_copy(q).start()
    chunk = rows.shape[0] // STORE_CHUNKS

    def rows_copy(c):
        r = pl.ds(c * chunk, chunk)
        return pltpu.make_async_copy(rows.at[r, :], rows_v.at[r, :], rows_sem.at[c])

    for c in range(STORE_CHUNKS):
        rows_copy(c).start()

    barrier = pltpu.get_barrier_semaphore()
    peers = []
    for k in range(1, T):
        peers.append((lax.rem(t + k, T), s))
    for d in range(1, S):
        for k in range(T):
            peers.append((lax.rem(t + k, T), lax.rem(s + d, S)))
    for pt, ps in peers:
        pl.semaphore_signal(barrier, inc=1, device_id={"tensor": pt, "store": ps}, device_id_type=MESH)

    total = None
    for c, (a, b) in enumerate(loads_g):
        cols = pl.ds(c * width, width)
        a.wait()
        b.wait()
        term = dot_nt(fout_v[:, cols], grads_v[:, cols])
        total = term if total is None else total + term
    outer_v[t] = total.astype(jnp.bfloat16)
    pl.semaphore_wait(barrier, len(peers))

    def gather_copy(slot, to, n):
        return pltpu.make_async_remote_copy(
            src_ref=outer_v.at[slot], dst_ref=outer_v.at[slot],
            send_sem=g_send.at[n], recv_sem=g_recv.at[slot],
            device_id={"tensor": to}, device_id_type=MESH,
        )

    partner = hi * 2 + (1 - lo)
    half = T // 2
    sends = []
    for k in range(1, half):
        sends.append(gather_copy(t, lax.rem(hi + k, half) * 2 + lo, len(sends)))
    sends.append(gather_copy(t, partner, len(sends)))
    for c in sends:
        c.start()

    for c in loads_f:
        c.wait()

    def project(q, _):
        act_copy(q).wait()
        r = pl.ds(pl.multiple_of(q * UTT_LEN, UTT_LEN), UTT_LEN)
        proj_v[r, :] = dot_nt(act_v[r, :], fin_v[...]).astype(jnp.bfloat16)
        return 0

    lax.fori_loop(0, FORWARD_AFTER, project, 0)
    for k in range(1, half):
        slot = lax.rem(hi + k, half) * 2 + lo
        c = gather_copy(slot, partner, len(sends))
        c.wait_recv()
        c.start()
        sends.append(c)
    lax.fori_loop(FORWARD_AFTER, count, project, 0)
    for k in range(half):
        gather_copy(lax.rem(hi + k, half) * 2 + (1 - lo), partner, 0).wait_recv()

    blocks = UTT_LEN // block
    per_utt = RANK // own
    lane = lax.broadcasted_iota(jnp.int32, (packed, PACK * RANK), 1)

    def partial(owner):
        q = owner // per_utt
        a0 = pl.multiple_of(lax.rem(owner, per_utt) * own, own)
        acc = None
        for i in range(blocks):
            left = outer_v[q * blocks + i, pl.ds(a0, own), :]
            right = proj_v[pl.ds(pl.multiple_of((q * blocks + i) * block, block), block), :]
            term = jnp.dot(left, right, preferred_element_type=jnp.float32)
            acc = term if acc is None else acc + term
        part_v[...] = acc
        even = part_v[pl.ds(0, packed, stride=2), :]
        odd = part_v[pl.ds(1, packed, stride=2), :]
        return jnp.where(lane < RANK, even, odd)

    reduce_copies = []
    for k in range(1, T):
        to = lax.rem(t + k, T)
        send_v[to] = partial(to).astype(jnp.bfloat16)
        c = pltpu.make_async_remote_copy(
            src_ref=send_v.at[to], dst_ref=recv_v.at[t],
            send_sem=r_send.at[to], recv_sem=r_recv.at[t],
            device_id={"tensor": to}, device_id_type=MESH,
        )
        c.start()
        reduce_copies.append(c)
    tmp_v[...] = partial(t)
    for k in range(1, T):
        src = lax.rem(t + k, T)
        pltpu.make_async_remote_copy(
            src_ref=send_v.at[src], dst_ref=recv_v.at[src],
            send_sem=r_send.at[src], recv_sem=r_recv.at[src],
            device_id={"tensor": src}, device_id_type=MESH,
        ).wait_recv()
        tmp_v[...] += recv_v[src].astype(jnp.float32)
    me = s * T + t
    every_v[me] = (tmp_v[...] * (1.0 / UTT_LEN ** 0.5)).astype(jnp.bfloat16)

    def every_copy(pt, ps, slot):
        return pltpu.make_async_remote_copy(
            src_ref=every_v.at[slot], dst_ref=every_v.at[slot],
            send_sem=e_send.at[ps * T + pt], recv_sem=e_recv.at[slot],
            device_id={"tensor": pt, "store": ps}, device_id_type=MESH,
        )

    every_sends = [every_copy(pt, ps, me) for pt, ps in peers]
    for c in every_sends:
        c.start()
    for pt, ps in peers:
        every_copy(pt, ps, ps * T + pt).wait_recv()
    wide_v[...] = every_v[...].reshape(S * T * packed, PACK * RANK).astype(jnp.float32)
    lines = RANK // PACK
    for j in range(lines):
        sk_v[:, pl.ds(j * PACK * RANK, PACK * RANK)] = wide_v[
            pl.ds(j, S * count, stride=lines), :
        ].astype(jnp.bfloat16)
    for c in range(STORE_CHUNKS):
        rows_copy(c).wait()
        r = pl.ds(c * chunk, chunk)
        out[:, r] = dot_nt(rows_v[r, :], sk_v[...]).T

    for c in sends + reduce_copies + every_sends:
        c.wait_send()


def solution(mesh):
    T, S = mesh.shape["tensor"], mesh.shape["store"]

    def shards(activations, out_grads, factor_in, factor_out, store_rows):
        tokens, width = activations.shape
        block, out_width = out_grads.shape
        n_rows, sketch = store_rows.shape
        count = tokens // UTT_LEN
        own = count * RANK // T
        packed = own // PACK
        lanes = PACK * RANK
        bf, f32 = jnp.bfloat16, jnp.float32
        dma = pltpu.SemaphoreType.DMA
        flops = 2 * RANK * (tokens * width + block * out_width) + 2 * S * count * n_rows * sketch
        moved = 2 * (activations.size + out_grads.size + store_rows.size)
        return pl.pallas_call(
            functools.partial(kernel, T, S),
            out_shape=jax.ShapeDtypeStruct((S * count, n_rows), f32),
            in_specs=[pl.BlockSpec(memory_space=pl.ANY)] * 5,
            out_specs=pl.BlockSpec(memory_space=pltpu.VMEM),
            scratch_shapes=[
                pltpu.VMEM((tokens, width), bf),
                pltpu.VMEM((block, out_width), bf),
                pltpu.VMEM((lanes, width), bf),
                pltpu.VMEM((RANK, out_width), bf),
                pltpu.VMEM((n_rows, sketch), bf),
                pltpu.VMEM((tokens, lanes), bf),
                pltpu.VMEM((T, RANK, block), bf),
                pltpu.VMEM((own, lanes), f32),
                pltpu.VMEM((T, packed, lanes), bf),
                pltpu.VMEM((T, packed, lanes), bf),
                pltpu.VMEM((S * T, packed, lanes), bf),
                pltpu.VMEM((S * T * packed, lanes), f32),
                pltpu.VMEM((S * count, sketch), bf),
                pltpu.VMEM((packed, lanes), f32),
                dma((count,)), dma((GRAD_CHUNKS,)), dma((PACK,)), dma((GRAD_CHUNKS,)), dma((STORE_CHUNKS,)),
                dma((T,)), dma((T,)), dma((T,)), dma((T,)), dma((S * T,)), dma((S * T,)),
            ],
            compiler_params=pltpu.CompilerParams(
                collective_id=0, has_side_effects=True, vmem_limit_bytes=63 * 2**20
            ),
            cost_estimate=pl.CostEstimate(flops=flops, bytes_accessed=moved, transcendentals=0),
            name="sketch_scores",
        )(activations, out_grads, factor_in.T, factor_out.T, store_rows)

    in_specs = (
        P(("groups", "store"), "tensor"),
        P(("groups", "store", "tensor"), None),
        P("tensor", None),
        P(),
        P(("groups", "tensor", "store"), None),
    )
    out_specs = P("groups", ("tensor", "store"))
    return jax.shard_map(shards, mesh=mesh, in_specs=in_specs, out_specs=out_specs, check_vma=False)
```

time: 101 us -> 40.7 us (0.40)
  blocking collectives: 77.9 us -> 0 us
  Pallas kernels: 0 us -> 39 us
  matrix products: 22.1 us -> 0 us
  local copies, waits for them, and re-layouts: 0.22 us -> 1.54 us
    psum x1 -> x0, blocking collectives: 45.2 us -> none  [shards(): summed = lax.psum(proj_in, 'tensor')]
    pallas_call x0 -> x1, Pallas kernels: none -> 39 us  [shards(): pl.pallas_call(functools.partial(kernel, T, S), out_shape=jax.ShapeDtypeS...]
    all_gather x2 -> x0, blocking collectives: 32.6 us -> none  [the longest x1 30.7 us: shards(): outer_all = lax.all_gather(proj_out, 'tensor', axis=0, tiled=True)]
    dot_general x4 -> x0, matrix products: 22.1 us -> none  [the longest x1 9.77 us: shards(): jnp.dot(activations, factor_in, preferred_element_type=jnp.float32)]
    unnamed x2 -> x1, local copies, waits for them, and re-layouts: 0.01 us -> 1.54 us
where the time goes in v1:
time: 40.7 us; the launch traced here: 40.5 us
  Pallas kernels  39 us (96%)
  local copies, waits for them, and re-layouts  1.54 us (4%)
    pallas_call x1, Pallas kernels, shards(): pl.pallas_call(functools.partial(kernel, T, S), out_shape=jax.ShapeDtypeS...  39 us
    unnamed x1, local copies, waits for them, and re-layouts  1.54 us

profile of v1, /device:TPU:0, one launch (start us, length us, event | category | flops | bytes accessed | tf_op | source)
XLA Modules:
  0.0 40.5 jit_solution(3010513053014722561)
XLA Ops:
  0.0 39.0 %sketch_scores.1 = f32[16,1536]{1,0:T(8,128)} custom-call(bf16[2048,3584]{1,0:T(8,128)(2,1)} %act.1, bf16[256,8192]{1,0:T(8,128)(2,1)} %grads.1, bf16[64,3584]{1,0:T(8,128)(2,1)} %bitcast.3, bf16[64,8192]{1,0:T(8,128)(2,1)} %bitcast.2, bf16[1536,4096]{1,0:T(8,128)(2,1)} %rows.1), custom_call_target="tpu_custom_call" | custom-call | flops 1409286144 | bytes 31457280 | tf_op jit(solution)/shard_map/sketch_scores/pallas_call | solution.py:211
  39.0 1.5 %copy.7 = f32[16,1536]{1,0:T(8,128)} copy(f32[16,1536]{1,0:T(8,128)} %sketch_scores.1) | data formatting | bytes 196608

commit v2 on v1

--- a/solution.py
+++ b/solution.py
@@ -12,7 +12,6 @@
 PACK = 128 // RANK
 STORE_CHUNKS = 4
 GRAD_CHUNKS = 2
-FORWARD_AFTER = 4
 MESH = pl.DeviceIdType.MESH
 NT = (((1,), (1,)), ((), ()))
 
@@ -24,7 +23,7 @@
 def kernel(
     T, S,
     act, grads, fin, fout, rows, out,
-    act_v, grads_v, fin_v, fout_v, rows_v, proj_v, outer_v, part_v, send_v, recv_v, every_v, wide_v, sk_v, tmp_v,
+    act_v, grads_v, fin_v, fout_v, rows_v, proj_v, outer_v, part_v, send_v, recv_v, every_v, wide_v, sk_v,
     act_sem, grads_sem, fin_sem, fout_sem, rows_sem,
     g_send, g_recv, r_send, r_recv, e_send, e_recv,
 ):
@@ -35,7 +34,6 @@
     block = grads.shape[0]
     own = count * RANK // T
     packed = own // PACK
-    lo, hi = lax.rem(t, 2), t // 2
 
     width = grads.shape[1] // GRAD_CHUNKS
     loads_g = []
@@ -66,9 +64,6 @@
         r = pl.ds(c * chunk, chunk)
         return pltpu.make_async_copy(rows.at[r, :], rows_v.at[r, :], rows_sem.at[c])
 
-    for c in range(STORE_CHUNKS):
-        rows_copy(c).start()
-
     barrier = pltpu.get_barrier_semaphore()
     peers = []
     for k in range(1, T):
@@ -96,12 +91,9 @@
             device_id={"tensor": to}, device_id_type=MESH,
         )
 
-    partner = hi * 2 + (1 - lo)
-    half = T // 2
     sends = []
-    for k in range(1, half):
-        sends.append(gather_copy(t, lax.rem(hi + k, half) * 2 + lo, len(sends)))
-    sends.append(gather_copy(t, partner, len(sends)))
+    for k in range(1, T):
+        sends.append(gather_copy(t, lax.rem(t + k, T), len(sends)))
     for c in sends:
         c.start()
 
@@ -114,57 +106,56 @@
         proj_v[r, :] = dot_nt(act_v[r, :], fin_v[...]).astype(jnp.bfloat16)
         return 0
 
-    lax.fori_loop(0, FORWARD_AFTER, project, 0)
-    for k in range(1, half):
-        slot = lax.rem(hi + k, half) * 2 + lo
-        c = gather_copy(slot, partner, len(sends))
-        c.wait_recv()
-        c.start()
-        sends.append(c)
-    lax.fori_loop(FORWARD_AFTER, count, project, 0)
-    for k in range(half):
-        gather_copy(lax.rem(hi + k, half) * 2 + (1 - lo), partner, 0).wait_recv()
+    lax.fori_loop(0, count // 2, project, 0)
+    for c in range(STORE_CHUNKS):
+        rows_copy(c).start()
+    lax.fori_loop(count // 2, count, project, 0)
+    for k in range(1, T):
+        gather_copy(lax.rem(t + k, T), t, 0).wait_recv()
 
     blocks = UTT_LEN // block
     per_utt = RANK // own
     lane = lax.broadcasted_iota(jnp.int32, (packed, PACK * RANK), 1)
 
-    def partial(owner):
-        q = owner // per_utt
-        a0 = pl.multiple_of(lax.rem(owner, per_utt) * own, own)
-        acc = None
-        for i in range(blocks):
-            left = outer_v[q * blocks + i, pl.ds(a0, own), :]
-            right = proj_v[pl.ds(pl.multiple_of((q * blocks + i) * block, block), block), :]
-            term = jnp.dot(left, right, preferred_element_type=jnp.float32)
-            acc = term if acc is None else acc + term
-        part_v[...] = acc
-        even = part_v[pl.ds(0, packed, stride=2), :]
-        odd = part_v[pl.ds(1, packed, stride=2), :]
-        return jnp.where(lane < RANK, even, odd)
-
-    reduce_copies = []
-    for k in range(1, T):
-        to = lax.rem(t + k, T)
-        send_v[to] = partial(to).astype(jnp.bfloat16)
-        c = pltpu.make_async_remote_copy(
-            src_ref=send_v.at[to], dst_ref=recv_v.at[t],
-            send_sem=r_send.at[to], recv_sem=r_recv.at[t],
+    def reduce_copy(to, src):
+        return pltpu.make_async_remote_copy(
+            src_ref=send_v.at[to], dst_ref=recv_v.at[src],
+            send_sem=r_send.at[to], recv_sem=r_recv.at[src],
             device_id={"tensor": to}, device_id_type=MESH,
         )
-        c.start()
-        reduce_copies.append(c)
-    tmp_v[...] = partial(t)
+
+    def partial(q, _):
+        for i in range(per_utt):
+            owner = q * per_utt + i
+            acc = None
+            for n in range(blocks):
+                left = outer_v[q * blocks + n, pl.ds(i * own, own), :]
+                right = proj_v[pl.ds(pl.multiple_of((q * blocks + n) * block, block), block), :]
+                term = jnp.dot(left, right, preferred_element_type=jnp.float32)
+                acc = term if acc is None else acc + term
+            part_v[...] = acc
+            even = part_v[pl.ds(0, packed, stride=2), :]
+            odd = part_v[pl.ds(1, packed, stride=2), :]
+            mine = jnp.where(lane < RANK, even, odd).astype(jnp.bfloat16)
+
+            @pl.when(owner != t)
+            def _():
+                send_v[owner] = mine
+                reduce_copy(owner, t).start()
+
+            @pl.when(owner == t)
+            def _():
+                recv_v[t] = mine
+        return 0
+
+    lax.fori_loop(0, count, partial, 0)
+
     for k in range(1, T):
         src = lax.rem(t + k, T)
-        pltpu.make_async_remote_copy(
-            src_ref=send_v.at[src], dst_ref=recv_v.at[src],
-            send_sem=r_send.at[src], recv_sem=r_recv.at[src],
-            device_id={"tensor": src}, device_id_type=MESH,
-        ).wait_recv()
-        tmp_v[...] += recv_v[src].astype(jnp.float32)
+        reduce_copy(src, src).wait_recv()
+    summed = jnp.sum(recv_v[...].astype(jnp.float32), axis=0)
     me = s * T + t
-    every_v[me] = (tmp_v[...] * (1.0 / UTT_LEN ** 0.5)).astype(jnp.bfloat16)
+    every_v[me] = (summed * (1.0 / UTT_LEN ** 0.5)).astype(jnp.bfloat16)
 
     def every_copy(pt, ps, slot):
         return pltpu.make_async_remote_copy(
@@ -186,10 +177,11 @@
         ].astype(jnp.bfloat16)
     for c in range(STORE_CHUNKS):
         rows_copy(c).wait()
-        r = pl.ds(c * chunk, chunk)
-        out[:, r] = dot_nt(rows_v[r, :], sk_v[...]).T
-
-    for c in sends + reduce_copies + every_sends:
+    out[...] = dot_nt(rows_v[...], sk_v[...]).T
+
+    for k in range(1, T):
+        reduce_copy(lax.rem(t + k, T), t).wait_send()
+    for c in sends + every_sends:
         c.wait_send()
 
 
@@ -227,7 +219,6 @@
                 pltpu.VMEM((S * T, packed, lanes), bf),
                 pltpu.VMEM((S * T * packed, lanes), f32),
                 pltpu.VMEM((S * count, sketch), bf),
-                pltpu.VMEM((packed, lanes), f32),
                 dma((count,)), dma((GRAD_CHUNKS,)), dma((PACK,)), dma((GRAD_CHUNKS,)), dma((STORE_CHUNKS,)),
                 dma((T,)), dma((T,)), dma((T,)), dma((T,)), dma((S * T,)), dma((S * T,)),
             ],

time: 40.7 us -> 33.8 us (0.83)
  Pallas kernels: 39 us -> 32.1 us
    pallas_call x1, Pallas kernels: 39 us -> 32.1 us  [shards(): pl.pallas_call(functools.partial(kernel, T, S), out_shape=jax.ShapeDtypeS...]
where the time goes in v2:
time: 33.8 us; the launch traced here: 33.7 us
  Pallas kernels  32.1 us (95%)
  local copies, waits for them, and re-layouts  1.54 us (5%)
    pallas_call x1, Pallas kernels, shards(): pl.pallas_call(functools.partial(kernel, T, S), out_shape=jax.ShapeDtypeS...  32.1 us
    unnamed x1, local copies, waits for them, and re-layouts  1.54 us

profile of v2, /device:TPU:0, one launch (start us, length us, event | category | flops | bytes accessed | tf_op | source)
XLA Modules:
  0.0 33.7 jit_solution(15691701938852515944)
XLA Ops:
  0.0 32.1 %sketch_scores.1 = f32[16,1536]{1,0:T(8,128)} custom-call(bf16[2048,3584]{1,0:T(8,128)(2,1)} %act.1, bf16[256,8192]{1,0:T(8,128)(2,1)} %grads.1, bf16[64,3584]{1,0:T(8,128)(2,1)} %bitcast.3, bf16[64,8192]{1,0:T(8,128)(2,1)} %bitcast.2, bf16[1536,4096]{1,0:T(8,128)(2,1)} %rows.1), custom_call_target="tpu_custom_call" | custom-call | flops 1409286144 | bytes 31457280 | tf_op jit(solution)/shard_map/sketch_scores/pallas_call | solution.py:203
  32.1 1.5 %copy.7 = f32[16,1536]{1,0:T(8,128)} copy(f32[16,1536]{1,0:T(8,128)} %sketch_scores.1) | data formatting | bytes 196608

commit v3 on v2

--- a/solution.py
+++ b/solution.py
@@ -32,8 +32,11 @@
     tokens = act.shape[0]
     count = tokens // UTT_LEN
     block = grads.shape[0]
-    own = count * RANK // T
-    packed = own // PACK
+    owners, first = T // 2, T // 4
+    per = count // owners
+    packed = RANK // PACK
+    mine = t - first
+    is_owner = (t >= first) & (t < first + owners)
 
     width = grads.shape[1] // GRAD_CHUNKS
     loads_g = []
@@ -114,62 +117,64 @@
         gather_copy(lax.rem(t + k, T), t, 0).wait_recv()
 
     blocks = UTT_LEN // block
-    per_utt = RANK // own
     lane = lax.broadcasted_iota(jnp.int32, (packed, PACK * RANK), 1)
 
-    def reduce_copy(to, src):
+    def reduce_copy(q, src):
         return pltpu.make_async_remote_copy(
-            src_ref=send_v.at[to], dst_ref=recv_v.at[src],
-            send_sem=r_send.at[to], recv_sem=r_recv.at[src],
-            device_id={"tensor": to}, device_id_type=MESH,
+            src_ref=send_v.at[q], dst_ref=recv_v.at[lax.rem(q, per), src],
+            send_sem=r_send.at[q], recv_sem=r_recv.at[lax.rem(q, per) * T + src],
+            device_id={"tensor": first + q // per}, device_id_type=MESH,
         )
 
     def partial(q, _):
-        for i in range(per_utt):
-            owner = q * per_utt + i
-            acc = None
-            for n in range(blocks):
-                left = outer_v[q * blocks + n, pl.ds(i * own, own), :]
-                right = proj_v[pl.ds(pl.multiple_of((q * blocks + n) * block, block), block), :]
-                term = jnp.dot(left, right, preferred_element_type=jnp.float32)
-                acc = term if acc is None else acc + term
-            part_v[...] = acc
-            even = part_v[pl.ds(0, packed, stride=2), :]
-            odd = part_v[pl.ds(1, packed, stride=2), :]
-            mine = jnp.where(lane < RANK, even, odd).astype(jnp.bfloat16)
-
-            @pl.when(owner != t)
-            def _():
-                send_v[owner] = mine
-                reduce_copy(owner, t).start()
-
-            @pl.when(owner == t)
-            def _():
-                recv_v[t] = mine
+        acc = None
+        for n in range(blocks):
+            right = proj_v[pl.ds(pl.multiple_of((q * blocks + n) * block, block), block), :]
+            term = jnp.dot(outer_v[q * blocks + n], right, preferred_element_type=jnp.float32)
+            acc = term if acc is None else acc + term
+        part_v[...] = acc
+        even = part_v[pl.ds(0, packed, stride=2), :]
+        odd = part_v[pl.ds(1, packed, stride=2), :]
+        value = jnp.where(lane < RANK, even, odd).astype(jnp.bfloat16)
+        home = first + q // per
+
+        @pl.when(home != t)
+        def _():
+            send_v[q] = value
+            reduce_copy(q, t).start()
+
+        @pl.when(home == t)
+        def _():
+            recv_v[lax.rem(q, per), t] = value
         return 0
 
     lax.fori_loop(0, count, partial, 0)
 
-    for k in range(1, T):
-        src = lax.rem(t + k, T)
-        reduce_copy(src, src).wait_recv()
-    summed = jnp.sum(recv_v[...].astype(jnp.float32), axis=0)
-    me = s * T + t
-    every_v[me] = (summed * (1.0 / UTT_LEN ** 0.5)).astype(jnp.bfloat16)
-
-    def every_copy(pt, ps, slot):
+    def every_copy(pt, ps, o, os):
+        slots = pl.ds(os * count + o * per, per)
         return pltpu.make_async_remote_copy(
-            src_ref=every_v.at[slot], dst_ref=every_v.at[slot],
-            send_sem=e_send.at[ps * T + pt], recv_sem=e_recv.at[slot],
+            src_ref=every_v.at[slots], dst_ref=every_v.at[slots],
+            send_sem=e_send.at[ps * T + pt], recv_sem=e_recv.at[os * owners + o],
             device_id={"tensor": pt, "store": ps}, device_id_type=MESH,
         )
 
-    every_sends = [every_copy(pt, ps, me) for pt, ps in peers]
-    for c in every_sends:
-        c.start()
-    for pt, ps in peers:
-        every_copy(pt, ps, ps * T + pt).wait_recv()
-    wide_v[...] = every_v[...].reshape(S * T * packed, PACK * RANK).astype(jnp.float32)
+    @pl.when(is_owner)
+    def _():
+        for j in range(per):
+            for k in range(1, T):
+                reduce_copy(j, lax.rem(t + k, T)).wait_recv()
+        for j in range(per):
+            summed = jnp.sum(recv_v[j].astype(jnp.float32), axis=0)
+            every_v[s * count + mine * per + j] = (summed * (1.0 / UTT_LEN ** 0.5)).astype(jnp.bfloat16)
+        for pt, ps in peers:
+            every_copy(pt, ps, mine, s).start()
+
+    for os in range(S):
+        for o in range(owners):
+            @pl.when((s != os) | (t != first + o))
+            def _():
+                every_copy(t, s, o, os).wait_recv()
+    wide_v[...] = every_v[...].reshape(S * count * packed, PACK * RANK).astype(jnp.float32)
     lines = RANK // PACK
     for j in range(lines):
         sk_v[:, pl.ds(j * PACK * RANK, PACK * RANK)] = wide_v[
@@ -179,9 +184,17 @@
         rows_copy(c).wait()
     out[...] = dot_nt(rows_v[...], sk_v[...]).T
 
-    for k in range(1, T):
-        reduce_copy(lax.rem(t + k, T), t).wait_send()
-    for c in sends + every_sends:
+    for q in range(count):
+        @pl.when(t != first + q // per)
+        def _():
+            reduce_copy(q, t).wait_send()
+
+    @pl.when(is_owner)
+    def _():
+        for pt, ps in peers:
+            every_copy(pt, ps, mine, s).wait_send()
+
+    for c in sends:
         c.wait_send()
 
 
@@ -193,8 +206,8 @@
         block, out_width = out_grads.shape
         n_rows, sketch = store_rows.shape
         count = tokens // UTT_LEN
-        own = count * RANK // T
-        packed = own // PACK
+        packed = RANK // PACK
+        per = count // (T // 2)
         lanes = PACK * RANK
         bf, f32 = jnp.bfloat16, jnp.float32
         dma = pltpu.SemaphoreType.DMA
@@ -213,14 +226,14 @@
                 pltpu.VMEM((n_rows, sketch), bf),
                 pltpu.VMEM((tokens, lanes), bf),
                 pltpu.VMEM((T, RANK, block), bf),
-                pltpu.VMEM((own, lanes), f32),
-                pltpu.VMEM((T, packed, lanes), bf),
-                pltpu.VMEM((T, packed, lanes), bf),
-                pltpu.VMEM((S * T, packed, lanes), bf),
-                pltpu.VMEM((S * T * packed, lanes), f32),
+                pltpu.VMEM((RANK, lanes), f32),
+                pltpu.VMEM((count, packed, lanes), bf),
+                pltpu.VMEM((per, T, packed, lanes), bf),
+                pltpu.VMEM((S * count, packed, lanes), bf),
+                pltpu.VMEM((S * count * packed, lanes), f32),
                 pltpu.VMEM((S * count, sketch), bf),
                 dma((count,)), dma((GRAD_CHUNKS,)), dma((PACK,)), dma((GRAD_CHUNKS,)), dma((STORE_CHUNKS,)),
-                dma((T,)), dma((T,)), dma((T,)), dma((T,)), dma((S * T,)), dma((S * T,)),
+                dma((T,)), dma((T,)), dma((count,)), dma((per * T,)), dma((S * T,)), dma((S * T,)),
             ],
             compiler_params=pltpu.CompilerParams(
                 collective_id=0, has_side_effects=True, vmem_limit_bytes=63 * 2**20

time: 33.8 us -> 33.1 us (0.979)
  Pallas kernels: 32.1 us -> 31.4 us
    pallas_call x1, Pallas kernels: 32.1 us -> 31.4 us  [shards(): pl.pallas_call(functools.partial(kernel, T, S), out_shape=jax.ShapeDtypeS...]
where the time goes in v3:
time: 33.1 us; the launch traced here: 33 us
  Pallas kernels  31.4 us (95%)
  local copies, waits for them, and re-layouts  1.54 us (5%)
    pallas_call x1, Pallas kernels, shards(): pl.pallas_call(functools.partial(kernel, T, S), out_shape=jax.ShapeDtypeS...  31.4 us
    unnamed x1, local copies, waits for them, and re-layouts  1.54 us

profile of v3, /device:TPU:0, one launch (start us, length us, event | category | flops | bytes accessed | tf_op | source)
XLA Modules:
  0.0 33.0 jit_solution(5898749753712006869)
XLA Ops:
  0.0 31.4 %sketch_scores.1 = f32[16,1536]{1,0:T(8,128)} custom-call(bf16[2048,3584]{1,0:T(8,128)(2,1)} %act.1, bf16[256,8192]{1,0:T(8,128)(2,1)} %grads.1, bf16[64,3584]{1,0:T(8,128)(2,1)} %bitcast.3, bf16[64,8192]{1,0:T(8,128)(2,1)} %bitcast.2, bf16[1536,4096]{1,0:T(8,128)(2,1)} %rows.1), custom_call_target="tpu_custom_call" | custom-call | flops 1409286144 | bytes 31457280 | tf_op jit(solution)/shard_map/sketch_scores/pallas_call | solution.py:216
  31.4 1.5 %copy.7 = f32[16,1536]{1,0:T(8,128)} copy(f32[16,1536]{1,0:T(8,128)} %sketch_scores.1) | data formatting | bytes 196608
